TPU v7x, 1024 devices: a whole 4x8x16 slice. The times are simulated.
1024 devices in a mesh: wide: 64 (over y, x, core), group: 16 (over z).
Axes of the slice: x: 4, y: 8, z: 16, core: 2. Of those that a mesh axis runs over, the one named last changes fastest.
Arguments:
- queries: bfloat16 [262144, 256], P(('wide', 'group')), may hold values from -100 to 100
- items: bfloat16 [262144, 256], P(('wide', 'group')), may hold values from -8 to 8
- cold_table: float32 [524288, 256], P(('wide', 'group')), may hold values from -6 to 6
- accum: float32 [524288, 256], P(('wide', 'group')), may hold values from 1e-09 to 1e-08
- send_rows: int32 [65536, 16], P(('wide', 'group')), may hold values from 0 to 511
- live_counts: int32 [1024, 64], P(('wide', 'group')), may hold values from 1 to 16, as said below
Outputs:
- query_grad: float32 [262144, 256], P(('wide', 'group'))
- item_grad: float32 [262144, 256], P(('wide', 'group'))
- new_table: float32 [524288, 256], P(('wide', 'group'))
Inputs may be any that keep to these rules, and one draw needn't show every extreme that they name: `live_counts`: one owner index, drawn afresh, has all 16 slots live for every device.
All inputs are finite; a program needn't handle non-finite values.
Results may differ from a plain program's by a relative error of at most 0.00525.
Values may be sent and summed in bfloat16 or wider, within the bound.
A program may use at most 32 MiB of HBM per device.

v0:
```python
import jax
import jax.numpy as jnp
from jax import lax
from jax.sharding import PartitionSpec as P


def on_device(queries, items, cold_table, accum, send_rows, live_counts):
    rows_here = queries.shape[0]
    depth = queries.shape[1]
    width = lax.axis_size("wide")
    slots = send_rows.shape[1]
    scale = depth ** (-0.5)
    member = lax.axis_index("group")
    contract_rows = (((0,), (0,)), ((), ()))
    contract_cols = (((1,), (1,)), ((), ()))
    fetched = cold_table[send_rows.reshape(-1)].astype(jnp.bfloat16).reshape(width, slots, depth)
    arrived = lax.all_to_all(fetched, "wide", split_axis=0, concat_axis=0, tiled=True)
    cold_keys = arrived.reshape(width * slots, depth)
    inbatch = lax.all_gather(items, "group", axis=0, tiled=True)
    line = inbatch.shape[0]
    live = (jnp.arange(slots)[None, :] < live_counts.reshape(width, 1)).reshape(1, width * slots)
    s_in = (
        lax.dot_general(queries, inbatch, contract_cols, preferred_element_type=jnp.float32) * scale
    )
    s_cold = (
        lax.dot_general(queries, cold_keys, contract_cols, preferred_element_type=jnp.float32)
        * scale
    )
    s_cold = jnp.where(live, s_cold, -jnp.inf)
    top = jnp.maximum(jnp.max(s_in, axis=1), jnp.max(s_cold, axis=1))
    total = jnp.sum(jnp.exp(s_in - top[:, None]), axis=1) + jnp.sum(
        jnp.exp(s_cold - top[:, None]), axis=1
    )
    lse = top + jnp.log(total)
    target = member * rows_here + jnp.arange(rows_here)
    onehot = (jnp.arange(line)[None, :] == target[:, None]).astype(jnp.float32)
    d_in = (jnp.exp(s_in - lse[:, None]) - onehot).astype(jnp.bfloat16)
    d_cold = jnp.exp(s_cold - lse[:, None]).astype(jnp.bfloat16)
    query_grad = (
        jnp.dot(d_in, inbatch, preferred_element_type=jnp.float32)
        + jnp.dot(d_cold, cold_keys, preferred_element_type=jnp.float32)
    ) * scale
    slot_grads = (
        lax.dot_general(d_cold, queries, contract_rows, preferred_element_type=jnp.float32) * scale
    )
    returned = lax.all_to_all(
        slot_grads.reshape(width, slots, depth), "wide", split_axis=0, concat_axis=0, tiled=True
    )
    item_grad = lax.psum_scatter(
        lax.dot_general(d_in, queries, contract_rows, preferred_element_type=jnp.float32) * scale,
        "group",
        scatter_dimension=0,
        tiled=True,
    )
    grads = (
        jnp.zeros(cold_table.shape, jnp.float32)
        .at[send_rows.reshape(-1)]
        .add(returned.reshape(-1, depth))
    )
    new_accum = accum + grads * grads
    new_table = cold_table - 0.5 * grads / jnp.sqrt(new_accum)
    return (query_grad, item_grad, new_table)


def solution(mesh):
    return jax.shard_map(
        on_device,
        mesh=mesh,
        in_specs=(
            P(("wide", "group"), None),
            P(("wide", "group"), None),
            P(("wide", "group"), None),
            P(("wide", "group"), None),
            P(("wide", "group"), None),
            P(("wide", "group"), None),
        ),
        out_specs=(
            P(("wide", "group"), None),
            P(("wide", "group"), None),
            P(("wide", "group"), None),
        ),
        check_vma=False,
    )
```

profile of v0, /device:TPU:10, one launch (start us, length us, event | category | flops | bytes accessed | tf_op | source)
XLA Modules:
  0.0 189.8 jit_solution(5149515016454884090)
XLA Ops:
  7.2 0.0 copy-start
  7.2 0.0 copy-start.6
  7.2 0.0 all-gather.2.cloned.1.call-start
  7.2 0.7 all-gather.2.cloned.1.call-update
  7.9 0.8 copy.9
  8.7 0.1 reshape.87
  8.8 5.7 %gather_fusion = bf16[1024,256]{1,0:T(8,128)(2,1)} fusion(f32[512,256]{1,0:T(8,128)} %param.8, s32[1024]{0:T(1024)S(1)} %broadcast_clamp_fusion), kind=kCustom, calls=%fused_computation | custom fusion | bytes 1052672 | tf_op jit(solution)/shard_map/gather | solution.py:16
  14.5 17.2 %all-to-all-start = ((bf16[64,16,256]{2,1,0:T(8,128)(2,1)}), bf16[64,16,256]{2,1,0:T(8,128)(2,1)S(1)}, u32[]{:S(2)}, u32[]{:S(2)}) async-start(bf16[64,16,256]{2,1,0:T(8,128)(2,1)} %bitcast.2), calls=%async_computation | async-start | bytes 1048576 | tf_op jit(solution)/shard_map/all_to_all | solution.py:17
  31.7 0.0 reduce-scatter.2.cloned.1.call-start
  31.7 0.0 copy-done.6
  31.7 0.1 iota_compare_fusion.1
  31.8 0.1 lt.37
  31.9 16.5 %all-to-all-done = bf16[64,16,256]{2,1,0:T(8,128)(2,1)S(1)} async-done(((bf16[64,16,256]{2,1,0:T(8,128)(2,1)}), bf16[64,16,256]{2,1,0:T(8,128)(2,1)S(1)}, u32[]{:S(2)}, u32[]{:S(2)}) %all-to-all-start) | async-done | bytes 524320 | tf_op jit(solution)/shard_map/all_to_all | solution.py:17
  48.4 0.0 copy-start.4
  48.4 0.0 copy-done
  48.4 0.8 fusion.5
  49.2 0.0 copy-start.2
  49.2 46.3 %all-gather.2.cloned.1.call-done = bf16[4096,256]{1,0:T(8,128)(2,1)} async-done(((bf16[256,256]{1,0:T(8,128)(2,1)}), bf16[4096,256]{1,0:T(8,128)(2,1)}) %all-gather.2.cloned.1.call-update) | async-done | bytes 2097168 | tf_op jit(solution)/shard_map/all_gather | solution.py:19
  95.6 2.4 %fusion.4 = (f32[256]{0:T(256)S(1)}, f32[256,4096]{1,0:T(8,128)S(1)}) fusion(bf16[256,256]{1,0:T(8,128)(2,1)S(1)} %copy-done, bf16[4096,256]{1,0:T(8,128)(2,1)} %all-gather.2.cloned.1.call-done), kind=kOutput, calls=%fused_computation.22 | convolution fusion | flops 538967808 | bytes 6423552 | tf_op jit(solution)/shard_map/dot_general | solution.py:23
  98.0 0.2 exponential_reduce_fusion.1
  98.2 0.0 copy-done.4
  98.2 0.7 exponential_reduce_fusion
  99.0 1.3 subtract_convert_fusion
  100.2 2.7 %convolution_multiply_fusion = f32[4096,256]{1,0:T(8,128)} fusion(bf16[256,4096]{1,0:T(8,128)(2,1)S(1)} %subtract_convert_fusion, bf16[256,256]{1,0:T(8,128)(2,1)S(1)} %copy-done), kind=kOutput, calls=%fused_computation.2 | convolution fusion | flops 537919488 | bytes 6422528 | tf_op jit(solution)/shard_map/dot_general | solution.py:50
  103.0 0.0 reduce-scatter.2.cloned.1.call-update
  103.0 0.0 copy-done.2
  103.0 1.4 convolution_multiply_fusion.2
  104.4 0.0 copy-start.5
  104.4 0.0 copy-start.1
  104.4 10.4 %all-to-all-start.1 = ((f32[64,16,256]{2,1,0:T(8,128)}), f32[64,16,256]{2,1,0:T(8,128)}, u32[]{:S(2)}, u32[]{:S(2)}) async-start(f32[64,16,256]{2,1,0:T(8,128)} %bitcast.18), calls=%async_computation.2 | async-start | bytes 2097152 | tf_op jit(solution)/shard_map/all_to_all | solution.py:46
  114.8 0.0 copy-start.3
  114.8 2.4 %fusion.6 = f32[256,256]{1,0:T(8,128)S(1)} fusion(bf16[256,4096]{1,0:T(8,128)(2,1)S(1)} %subtract_convert_fusion, bf16[4096,256]{1,0:T(8,128)(2,1)} %all-gather.2.cloned.1.call-done), kind=kOutput, calls=%fused_computation.24 | convolution fusion | flops 536870912 | bytes 4456448 | tf_op jit(solution)/shard_map/dot_general | solution.py:40
  117.2 0.0 copy-done.5
  117.2 0.0 copy-done.3
  117.2 1.1 fusion.1
  118.3 24.4 %all-to-all-done.1 = f32[64,16,256]{2,1,0:T(8,128)} async-done(((f32[64,16,256]{2,1,0:T(8,128)}), f32[64,16,256]{2,1,0:T(8,128)}, u32[]{:S(2)}, u32[]{:S(2)}) %all-to-all-start.1) | async-done | bytes 1048608 | tf_op jit(solution)/shard_map/all_to_all | solution.py:46
  142.6 6.7 %scatter_custom_fusion = f32[512,256]{1,0:T(8,128)S(1)} fusion(s32[1024]{0:T(1024)S(1)} %bitcast.20, f32[1024,256]{1,0:T(8,128)} %bitcast.5, f32[]{:T(128)} %constant.12.clone.1), kind=kCustom, calls=%fused_computation.15 | custom fusion | flops 262144 | bytes 524800 | tf_op jit(solution)/shard_map/scatter-add | solution.py:58
  149.3 0.0 copy-done.1
  149.3 1.9 %multiply_subtract_fusion = f32[512,256]{1,0:T(8,128)} fusion(f32[512,256]{1,0:T(8,128)S(1)} %copy-done.1, f32[512,256]{1,0:T(8,128)} %param.9, f32[512,256]{1,0:T(8,128)S(1)} %scatter_custom_fusion), kind=kLoop, calls=%fused_computation.14 | loop fusion | flops 655360 | bytes 2097152 | tf_op jit(solution)/shard_map/sub | solution.py:61
  151.3 31.7 %reduce-scatter.2.cloned.1.call-done = f32[256,256]{1,0:T(8,128)} async-done(((f32[4096,256]{1,0:T(8,128)}), f32[256,256]{1,0:T(8,128)}) %reduce-scatter.2.cloned.1.call-update) | async-done | bytes 262160 | tf_op jit(solution)/shard_map/reduce_scatter | solution.py:49
  (5 shorter events, 0.0 us)
Async XLA Ops:
  7.2 41.3 %copy-start = (bf16[256,256]{1,0:T(8,128)(2,1)S(1)}, bf16[256,256]{1,0:T(8,128)(2,1)}, u32[]{:S(2)}) copy-start(bf16[256,256]{1,0:T(8,128)(2,1)} %param.6) | copy-start | bytes 393220
  7.2 24.6 %copy-start.6 = (s32[1,64]{1,0:T(1,128)S(1)}, s32[1,64]{1,0:T(1,128)}, u32[]{:S(2)}) copy-start(s32[1,64]{1,0:T(1,128)} %param.11) | copy-start | bytes 772
  7.2 88.4 %all-gather.2.cloned.1.call-start = ((), (), s32[]{:S(2)}) async-start(), calls=%async_computation.3 | async-start | bytes 2228224 | tf_op jit(solution)/shard_map/all_gather | solution.py:19
  14.5 34.0 %all-to-all-start = ((bf16[64,16,256]{2,1,0:T(8,128)(2,1)}), bf16[64,16,256]{2,1,0:T(8,128)(2,1)S(1)}, u32[]{:S(2)}, u32[]{:S(2)}) async-start(bf16[64,16,256]{2,1,0:T(8,128)(2,1)} %bitcast.2), calls=%async_computation | async-start | bytes 1048576 | tf_op jit(solution)/shard_map/all_to_all | solution.py:17
  31.7 151.3 %reduce-scatter.2.cloned.1.call-start = ((), (), s32[]{:S(2)}) async-start(), calls=%async_computation.4 | async-start | bytes 4456448 | tf_op jit(solution)/shard_map/reduce_scatter | solution.py:49
  48.4 49.8 %copy-start.4 = (bf16[64,16,256]{2,1,0:T(8,128)(2,1)}, bf16[64,16,256]{2,1,0:T(8,128)(2,1)S(1)}, u32[]{:S(2)}) copy-start(bf16[64,16,256]{2,1,0:T(8,128)(2,1)S(1)} %all-to-all-done) | copy-start | bytes 1572868
  49.2 53.8 %copy-start.2 = (f32[1024,256]{1,0:T(8,128)}, f32[1024,256]{1,0:T(8,128)S(1)}, u32[]{:S(2)}) copy-start(f32[1024,256]{1,0:T(8,128)S(1)} %get-tuple-element.6) | copy-start | bytes 3145732
  104.4 12.8 %copy-start.5 = (bf16[64,16,256]{2,1,0:T(8,128)(2,1)S(1)}, bf16[64,16,256]{2,1,0:T(8,128)(2,1)}, u32[]{:S(2)}) copy-start(bf16[64,16,256]{2,1,0:T(8,128)(2,1)} %copy-done.4) | copy-start | bytes 1572868
  104.4 45.0 %copy-start.1 = (f32[512,256]{1,0:T(8,128)S(1)}, f32[512,256]{1,0:T(8,128)}, u32[]{:S(2)}) copy-start(f32[512,256]{1,0:T(8,128)} %param.8) | copy-start | bytes 1572868
  104.4 38.3 %all-to-all-start.1 = ((f32[64,16,256]{2,1,0:T(8,128)}), f32[64,16,256]{2,1,0:T(8,128)}, u32[]{:S(2)}, u32[]{:S(2)}) async-start(f32[64,16,256]{2,1,0:T(8,128)} %bitcast.18), calls=%async_computation.2 | async-start | bytes 2097152 | tf_op jit(solution)/shard_map/all_to_all | solution.py:46
  114.8 2.4 %copy-start.3 = (f32[1024,256]{1,0:T(8,128)S(1)}, f32[1024,256]{1,0:T(8,128)}, u32[]{:S(2)}) copy-start(f32[1024,256]{1,0:T(8,128)} %copy-done.2) | copy-start | bytes 3145732
Sparse Core Ops, SparseCore 0:
  10.7 84.8 all-gather.1
  103.1 79.8 reduce-scatter.1
where the time goes:
time: 190 us
  waiting for transfers between devices  120 us (63%)
  starting transfers between devices  27.7 us (15%)
  between operations  14.2 us (7%)
  other arithmetic  10.9 us (6%)
  matrix products  10.7 us (6%)
  local copies, waits for them, and re-layouts  6.64 us (3%)
    all_gather x1, waiting for transfers between devices, on_device(): inbatch = lax.all_gather(items, 'group', axis=0, tiled=True)  46.3 us
    reduce_scatter x1, waiting for transfers between devices, on_device(): lax.psum_scatter(lax.dot_general(d_in, queries, contract_rows, preferred_...  31.7 us
    all_to_all x1, waiting for transfers between devices, on_device(): lax.all_to_all(slot_grads.reshape(width, slots, depth), 'wide', split_axi...  24.4 us
    all_to_all x1, starting transfers between devices, on_device(): lax.all_to_all(fetched, 'wide', split_axis=0, concat_axis=0, tiled=True)  17.2 us
    all_to_all x1, waiting for transfers between devices, on_device(): lax.all_to_all(fetched, 'wide', split_axis=0, concat_axis=0, tiled=True)  16.5 us
    all_to_all x1, starting transfers between devices, on_device(): lax.all_to_all(slot_grads.reshape(width, slots, depth), 'wide', split_axi...  10.4 us
    scatter-add x1, other arithmetic, on_device(): grads = jnp.zeros(cold_table.shape, jnp.float32).at[send_rows.reshape(-1)...  6.66 us
    gather x1, local copies, waits for them, and re-layouts, on_device(): cold_table[send_rows.reshape(-1)].astype(jnp.bfloat16)  5.65 us
  transfers between devices with their start and end apart: 4, of which 4 were waited for; matrix products, arithmetic and copies ran while one was open for 11% of the time, Pallas kernels for 0%

commit v1 on v0

v1 whole, which is shorter than its diff:
```python
import functools

import jax
import jax.numpy as jnp
from jax import lax
from jax.experimental import pallas as pl
from jax.experimental.pallas import tpu as pltpu
from jax.sharding import PartitionSpec as P

MESH = pl.DeviceIdType.MESH
NT = (((1,), (1,)), ((), ()))
TN = (((0,), (0,)), ((), ()))
F32 = jnp.float32
BF16 = jnp.bfloat16


def dot(a, b, dims=(((1,), (0,)), ((), ()))):
    return lax.dot_general(a, b, dims, preferred_element_type=F32)


def as_bf16(condition):
    return jnp.where(condition, 1.0, 0.0).astype(BF16)


def kernel(
    n_w,
    n_g,
    cap,
    queries,
    items,
    table_hbm,
    accum_hbm,
    send_rows,
    live_counts,
    query_grad,
    item_grad,
    new_table,
    keys,
    line_q,
    lse_all,
    s_in,
    s_cold,
    top8,
    sum8,
    table,
    accum,
    cold_out,
    cold_keys,
    slot_out,
    slot_back,
    query_t,
    load_sem,
    item_send,
    item_recv,
    q_send,
    q_recv,
    lse_send,
    lse_recv,
    wide_send,
    wide_recv,
):
    w, g = lax.axis_index("wide"), lax.axis_index("group")
    right, left = lax.rem(g + 1, n_g), lax.rem(g + n_g - 1, n_g)
    half = n_g // 2
    rows, depth = queries.shape
    chunk = rows // 2
    slots = n_w * cap
    table_rows = table.shape[0]
    scale = depth ** (-0.5)

    loads = [
        pltpu.make_async_copy(items, keys.at[0], load_sem.at[0]),
        pltpu.make_async_copy(queries, line_q.at[0], load_sem.at[1]),
        pltpu.make_async_copy(table_hbm, table, load_sem.at[2]),
        pltpu.make_async_copy(accum_hbm, accum, load_sem.at[3]),
    ]
    for load in loads:
        load.start()

    barrier = pltpu.get_barrier_semaphore()

    @pl.loop(1, n_g)
    def _(p):
        pl.semaphore_signal(
            barrier, inc=1, device_id=(w, lax.rem(g + p, n_g)), device_id_type=MESH
        )

    @pl.loop(1, n_w)
    def _(p):
        pl.semaphore_signal(
            barrier, inc=1, device_id=(lax.rem(w + p, n_w), g), device_id_type=MESH
        )

    def ring(buffer, send, recv, way, step, part):
        at = pl.ds(part * chunk, chunk)
        src, dst = (step - 1, step) if way == 0 else ((n_g + 1 - step) % n_g, n_g - step)
        return pltpu.make_async_remote_copy(
            src_ref=buffer.at[src, at],
            dst_ref=buffer.at[dst, at],
            send_sem=send.at[way, step, part],
            recv_sem=recv.at[way, step, part],
            device_id=(w, right if way == 0 else left),
            device_id_type=MESH,
        )

    def pieces(step):
        if isinstance(step, int) and step == half:
            return ((0, 0), (1, 1))
        return ((0, 0), (1, 0), (0, 1), (1, 1))

    def ring_start(buffer, send, recv, step):
        for way, part in pieces(step):
            ring(buffer, send, recv, way, step, part).start()

    def ring_pass(buffer, send, recv, step, last):
        for way, part in pieces(step):
            ring(buffer, send, recv, way, step, part).wait_recv()
            if not last or way == part:
                ring(buffer, send, recv, way, step + 1, part).start()

    def ring_end(buffer, send, recv):
        for way, part in pieces(half):
            ring(buffer, send, recv, way, half, part).wait_recv()

    def ring_drain(buffer, send, recv):
        @pl.loop(1, half)
        def _(step):
            for way, part in pieces(step):
                ring(buffer, send, recv, way, step, part).wait_send()

        for way, part in pieces(half):
            ring(buffer, send, recv, way, half, part).wait_send()

    item_ring = (keys, item_send, item_recv)
    query_ring = (line_q, q_send, q_recv)

    def wide_start(src, dst, k, peer):
        @pl.when(peer != w)
        def _():
            pltpu.make_async_remote_copy(
                src_ref=src.at[peer],
                dst_ref=dst.at[w],
                send_sem=wide_send.at[k],
                recv_sem=wide_recv.at[k],
                device_id=(peer, g),
                device_id_type=MESH,
            ).start()

        @pl.when(peer == w)
        def _():
            pltpu.make_async_copy(src.at[w], dst.at[w], wide_recv.at[k]).start()

    def wide_arrived(dst, k):
        pltpu.make_async_copy(dst, dst, wide_recv.at[k]).wait()

    def wide_drain(src, k):
        others = src.at[pl.ds(0, n_w - 1)]
        pltpu.make_async_copy(others, others, wide_send.at[k]).wait()

    owner = lax.broadcasted_iota(jnp.int32, (slots, n_w), 1)
    slot = lax.broadcasted_iota(jnp.int32, (slots, n_w), 0)
    spread = as_bf16(lax.div(slot, cap) == owner)
    picks = send_rows[...]
    high = (picks & ~15).astype(F32).astype(BF16)
    low = (picks & 15).astype(F32).astype(BF16)
    place = lax.broadcasted_iota(jnp.int32, (slots, cap), 1)
    slot = lax.broadcasted_iota(jnp.int32, (slots, cap), 0)
    mine = lax.rem(slot, cap) == place
    high = jnp.where(mine, dot(spread, high), 0.0).astype(BF16)
    low = jnp.where(mine, dot(spread, low), 0.0).astype(BF16)
    ones = jnp.ones((cap, table_rows), BF16)
    row_of = dot(high, ones) + dot(low, ones)
    row = lax.broadcasted_iota(jnp.int32, (slots, table_rows), 1).astype(F32)
    pick = as_bf16(row_of == row)
    loads[2].wait()
    fetched = dot(pick, table[...].astype(BF16)).astype(BF16)
    cold_out[...] = fetched.reshape(n_w, cap, depth)

    loads[0].wait()
    loads[1].wait()
    query_t[...] = jnp.transpose(line_q[0])

    pl.semaphore_wait(barrier, n_g - 1 + n_w - 1)
    ring_start(*item_ring, 1)

    @pl.loop(1, n_w + 1)
    def _(p):
        wide_start(cold_out, cold_keys, 0, lax.rem(w + p, n_w))

    def fold(s, first=False):
        s3 = s.reshape(s.shape[0] // 8, 8, s.shape[1])
        top = jnp.max(s3, axis=0)
        if first:
            top8[...] = top
            sum8[...] = jnp.sum(jnp.exp(s3 - top[None]), axis=0)
        else:
            before = top8[...]
            top = jnp.maximum(before, top)
            top8[...] = top
            sum8[...] = sum8[...] * jnp.exp(before - top) + jnp.sum(jnp.exp(s3 - top[None]), axis=0)

    def score(block, first=False):
        s = dot(keys[block], query_t[...]) * scale
        s_in[block] = s
        fold(s, first)

    score(0, first=True)

    cold_blocks = max(slots // 256, 1)
    cold_rows = slots // cold_blocks

    def score_cold(k):
        at = pl.ds(k * cold_rows, cold_rows)
        owner = lax.broadcasted_iota(jnp.int32, (cold_rows, n_w), 1)
        slot = lax.broadcasted_iota(jnp.int32, (cold_rows, n_w), 0) + k * cold_rows
        spread = as_bf16(lax.div(slot, cap) == owner)
        counts = jnp.broadcast_to(live_counts[...].astype(F32).astype(BF16), (rows, n_w))
        counts = dot(spread, counts, NT)
        place = lax.rem(lax.broadcasted_iota(jnp.int32, (cold_rows, rows), 0), cap).astype(F32)
        owners = pl.ds(k * (n_w // cold_blocks), n_w // cold_blocks)
        found = cold_keys[owners].reshape(cold_rows, depth)
        s = dot(found, query_t[...]) * scale
        s = jnp.where(place < counts, s, -jnp.inf)
        s_cold[at] = s
        fold(s)


    @pl.loop(1, half - 1)
    def _(step):
        ring_pass(*item_ring, step, False)
        score(step)
        score(n_g - step)

    ring_pass(*item_ring, half - 1, True)
    ring_start(*query_ring, 1)
    wide_arrived(cold_keys, 0)

    @pl.loop(0, cold_blocks)
    def _(k):
        score_cold(k)

    score(half - 1)
    if half > 1:
        score(half + 1)
    ring_end(*item_ring)
    score(half)

    top = jnp.max(top8[...], axis=0, keepdims=True)
    total = jnp.sum(sum8[...] * jnp.exp(top8[...] - top), axis=0, keepdims=True)
    lse_all[0] = top + jnp.log(total)

    def lse_copy(p):
        return pltpu.make_async_remote_copy(
            src_ref=lse_all.at[0],
            dst_ref=lse_all.at[p],
            send_sem=lse_send.at[p],
            recv_sem=lse_recv.at[p],
            device_id=(w, lax.rem(g + p, n_g)),
            device_id_type=MESH,
        )

    @pl.loop(1, n_g)
    def _(p):
        lse_copy(p).start()

    per = n_w // cold_blocks
    own_part = lax.div(w, per)

    @pl.loop(0, cold_blocks)
    def _(i):
        k = lax.rem(own_part + i, cold_blocks)
        at = pl.ds(pl.multiple_of(k * cold_rows, cold_rows), cold_rows)
        d = jnp.exp(s_cold[at] - lse_all[0]).astype(BF16)
        back = (dot(d, line_q[0]) * scale).astype(BF16)
        slot_out[pl.ds(k * per, per)] = back.reshape(per, cap, depth)

        @pl.loop(0, per)
        def _(j):
            wide_start(slot_out, slot_back, 1, k * per + lax.rem(w + j, per))

    ring_pass(*query_ring, 1, half == 2)

    d = jnp.exp(s_in[0] - lse_all[0])
    key = lax.broadcasted_iota(jnp.int32, d.shape, 0)
    query = lax.broadcasted_iota(jnp.int32, d.shape, 1)
    d = (d - jnp.where(key == query, 1.0, 0.0)).astype(BF16)
    query_grad[...] = dot(d, keys[0], TN)
    item_grad[...] = dot(d, line_q[0])

    def to_queries(block):
        d = jnp.exp(s_in[block] - lse_all[0]).astype(BF16)
        query_grad[...] += dot(d, keys[block], TN)

    def to_items(block):
        lse_copy(block).wait_recv()
        s = dot(keys[0], line_q[block], NT) * scale
        d = jnp.exp(s - lse_all[block]).astype(BF16)
        item_grad[...] += dot(d, line_q[block])

    @pl.loop(1, half - 1)
    def _(step):
        @pl.when(step > 1)
        def _():
            ring_pass(*query_ring, step, False)

        to_queries(step)
        to_queries(n_g - step)
        to_items(step)
        to_items(n_g - step)

    if half > 2:
        ring_pass(*query_ring, half - 1, True)
    to_queries(half - 1)
    to_queries(half)
    to_queries(half + 1)

    @pl.loop(0, cold_blocks)
    def _(k):
        d = jnp.exp(s_cold[pl.ds(k * cold_rows, cold_rows)] - lse_all[0]).astype(BF16)
        found = cold_keys[pl.ds(k * per, per)].reshape(cold_rows, depth)
        query_grad[...] += dot(d, found, TN)

    query_grad[...] = query_grad[...] * scale

    owner = lax.broadcasted_iota(jnp.int32, (n_w, slots), 0)
    slot = lax.broadcasted_iota(jnp.int32, (n_w, slots), 1)
    spread = as_bf16(lax.div(slot, cap) == owner)
    picks = send_rows[...]
    high = dot((picks & ~15).astype(F32).astype(BF16), spread, TN)
    low = dot((picks & 15).astype(F32).astype(BF16), spread, TN)
    place = lax.broadcasted_iota(jnp.int32, (cap, slots), 0)
    slot = lax.broadcasted_iota(jnp.int32, (cap, slots), 1)
    row_of = jnp.sum(
        jnp.where(lax.rem(slot, cap) == place, high + low, 0.0), axis=0, keepdims=True
    )
    row = lax.broadcasted_iota(jnp.int32, (table_rows, slots), 0).astype(F32)
    put = as_bf16(row_of == row)
    wide_arrived(slot_back, 1)
    loads[3].wait()
    grad = dot(put, slot_back[...].reshape(slots, depth))
    new_table[...] = table[...] - 0.5 * grad / jnp.sqrt(accum[...] + grad * grad)

    to_items(half - 1)
    to_items(half + 1)
    ring_end(*query_ring)
    to_items(half)
    item_grad[...] = item_grad[...] * scale

    wide_drain(cold_out, 0)
    wide_drain(slot_out, 1)

    @pl.loop(1, n_g)
    def _(p):
        lse_copy(p).wait_send()

    ring_drain(*item_ring)
    ring_drain(*query_ring)


def on_device(n_w, n_g, queries, items, cold_table, accum, send_rows, live_counts):
    rows, depth = queries.shape
    table_rows = cold_table.shape[0]
    cap = send_rows.shape[1]
    slots = n_w * cap
    half = n_g // 2
    vmem = pl.BlockSpec(memory_space=pltpu.VMEM)
    hbm = pl.BlockSpec(memory_space=pl.ANY)
    ring_sems = pltpu.SemaphoreType.DMA((2, half + 1, 2))
    return pl.pallas_call(
        functools.partial(kernel, n_w, n_g, cap),
        out_shape=(
            jax.ShapeDtypeStruct((rows, depth), F32),
            jax.ShapeDtypeStruct((rows, depth), F32),
            jax.ShapeDtypeStruct((table_rows, depth), F32),
        ),
        in_specs=[hbm, hbm, hbm, hbm, vmem, vmem],
        out_specs=(vmem, vmem, vmem),
        scratch_shapes=[
            pltpu.VMEM((n_g, rows, depth), BF16),
            pltpu.VMEM((n_g, rows, depth), BF16),
            pltpu.VMEM((n_g, 1, rows), F32),
            pltpu.VMEM((n_g, rows, rows), F32),
            pltpu.VMEM((slots, rows), F32),
            pltpu.VMEM((8, rows), F32),
            pltpu.VMEM((8, rows), F32),
            pltpu.VMEM((table_rows, depth), F32),
            pltpu.VMEM((table_rows, depth), F32),
            pltpu.VMEM((n_w, cap, depth), BF16),
            pltpu.VMEM((n_w, cap, depth), BF16),
            pltpu.VMEM((n_w, cap, depth), BF16),
            pltpu.VMEM((n_w, cap, depth), BF16),
            pltpu.VMEM((depth, rows), BF16),
            pltpu.SemaphoreType.DMA((4,)),
            ring_sems,
            ring_sems,
            ring_sems,
            ring_sems,
            pltpu.SemaphoreType.DMA((n_g,)),
            pltpu.SemaphoreType.DMA((n_g,)),
            pltpu.SemaphoreType.DMA((2,)),
            pltpu.SemaphoreType.DMA((2,)),
        ],
        compiler_params=pltpu.CompilerParams(
            collective_id=0, has_side_effects=True, vmem_limit_bytes=40 * 1024 * 1024
        ),
    )(queries, items, cold_table, accum, send_rows, live_counts)


def solution(mesh):
    spec = P(("wide", "group"), None)
    return jax.shard_map(
        functools.partial(on_device, mesh.shape["wide"], mesh.shape["group"]),
        mesh=mesh,
        in_specs=(spec,) * 6,
        out_specs=(spec,) * 3,
        check_vma=False,
    )
```

time: 190 us -> 97.8 us (0.51)
  the two profiles are of different devices: /device:TPU:10 before, /device:TPU:8 now
where the time goes in v1:
time: 97.8 us; the launch traced here: 97.4 us
  Pallas kernels  89.9 us (92%)
  local copies, waits for them, and re-layouts  6.87 us (7%)
    pallas_call x1, Pallas kernels, on_device(): pl.pallas_call(functools.partial(kernel, n_w, n_g, cap), out_shape=(jax.S...  89.9 us
    unnamed x14, local copies, waits for them, and re-layouts  6.87 us

profile of v1, /device:TPU:8, one launch (start us, length us, event | category | flops | bytes accessed | tf_op | source)
XLA Modules:
  0.0 97.4 jit_solution(8896349616867580993)
XLA Ops:
  0.6 0.0 copy-start.4
  0.6 0.8 copy.9.send_rows
  1.4 0.0 copy-done.4
  1.4 0.0 copy-start
  1.4 1.0 %copy-done = f32[512,256]{1,0:T(8,128)S(1)} copy-done((f32[512,256]{1,0:T(8,128)S(1)}, f32[512,256]{1,0:T(8,128)}, u32[]{:S(2)}) %copy-start) | copy-done | bytes 524312
  2.5 0.0 copy-start.1
  2.5 1.0 %copy-done.1 = f32[512,256]{1,0:T(8,128)S(1)} copy-done((f32[512,256]{1,0:T(8,128)S(1)}, f32[512,256]{1,0:T(8,128)}, u32[]{:S(2)}) %copy-start.1) | copy-done | bytes 524312
  3.5 0.0 copy-start.2
  3.5 0.9 copy-done.2
  4.4 0.0 copy-start.3
  4.4 0.9 copy-done.3
  5.3 89.9 %shard_map.85 = (f32[256,256]{1,0:T(8,128)S(1)}, f32[256,256]{1,0:T(8,128)S(1)}, f32[512,256]{1,0:T(8,128)S(1)}) custom-call(bf16[256,256]{1,0:T(8,128)(2,1)S(1)} %copy-done.2, bf16[256,256]{1,0:T(8,128)(2,1)S(1)} %copy-done.3, f32[512,256]{1,0:T(8,128)S(1)} %copy-done, f32[512,256]{1,0:T(8,128)S(1)} %copy-done.1, s32[64,16]{1,0:T(8,128)S(1)} %copy.9.send_rows, ...), custom_call_target="tpu_custom_call" | custom-call | tf_op jit(solution)/shard_map/pallas_call | solution.py:369
  95.2 0.7 copy.13
  96.0 0.7 copy.14
  96.7 0.8 copy.15
Async XLA Ops:
  0.6 0.8 copy-start.4
  1.4 1.0 %copy-start = (f32[512,256]{1,0:T(8,128)S(1)}, f32[512,256]{1,0:T(8,128)}, u32[]{:S(2)}) copy-start(f32[512,256]{1,0:T(8,128)} %table_hbm.1) | copy-start | bytes 1572868
  2.5 1.0 %copy-start.1 = (f32[512,256]{1,0:T(8,128)S(1)}, f32[512,256]{1,0:T(8,128)}, u32[]{:S(2)}) copy-start(f32[512,256]{1,0:T(8,128)} %accum_hbm.1) | copy-start | bytes 1572868
  3.5 0.9 copy-start.2
  4.4 0.9 copy-start.3

commit v2 on v1

v2 whole, which is shorter than its diff:
```python
import functools

import jax
import jax.numpy as jnp
from jax import lax
from jax.experimental import pallas as pl
from jax.experimental.pallas import tpu as pltpu
from jax.sharding import PartitionSpec as P

MESH = pl.DeviceIdType.MESH
NT = (((1,), (1,)), ((), ()))
TN = (((0,), (0,)), ((), ()))
F32 = jnp.float32
BF16 = jnp.bfloat16


def dot(a, b, dims=(((1,), (0,)), ((), ()))):
    return lax.dot_general(a, b, dims, preferred_element_type=F32)


def as_bf16(condition):
    return jnp.where(condition, 1.0, 0.0).astype(BF16)


def kernel(
    n_w,
    n_g,
    cap,
    queries,
    items,
    table_hbm,
    accum_hbm,
    send_rows,
    live_counts,
    query_grad_hbm,
    item_grad_hbm,
    new_table_hbm,
    query_grad,
    item_grad,
    new_table,
    keys,
    line_q,
    lse_all,
    s_in,
    s_back,
    s_cold,
    top8,
    sum8,
    table,
    accum,
    cold_out,
    cold_keys,
    slot_out,
    slot_back,
    query_t,
    put,
    load_sem,
    save_sem,
    ring_send,
    ring_recv,
    lse_send,
    lse_recv,
    wide_send,
    wide_recv,
):
    w, g = lax.axis_index("wide"), lax.axis_index("group")
    right, left = lax.rem(g + 1, n_g), lax.rem(g + n_g - 1, n_g)
    half = n_g // 2
    rows, depth = queries.shape
    chunk = rows // 2
    slots = n_w * cap
    table_rows = table.shape[0]
    scale = depth ** (-0.5)
    cold_blocks = max(slots // 256, 1)
    cold_rows = slots // cold_blocks

    loads = [
        pltpu.make_async_copy(items, keys.at[0], load_sem.at[0]),
        pltpu.make_async_copy(queries, line_q.at[0], load_sem.at[1]),
        pltpu.make_async_copy(table_hbm, table, load_sem.at[2]),
        pltpu.make_async_copy(accum_hbm, accum, load_sem.at[3]),
    ]
    for load in loads:
        load.start()

    saves = [
        pltpu.make_async_copy(query_grad, query_grad_hbm, save_sem.at[0]),
        pltpu.make_async_copy(item_grad, item_grad_hbm, save_sem.at[1]),
        pltpu.make_async_copy(new_table, new_table_hbm, save_sem.at[2]),
    ]

    barrier = pltpu.get_barrier_semaphore()

    @pl.loop(1, n_g)
    def _(p):
        pl.semaphore_signal(
            barrier, inc=1, device_id=(w, lax.rem(g + p, n_g)), device_id_type=MESH
        )

    @pl.loop(1, n_w)
    def _(p):
        pl.semaphore_signal(
            barrier, inc=1, device_id=(lax.rem(w + p, n_w), g), device_id_type=MESH
        )

    def ring(line, way, part, step):
        at = pl.ds(part * chunk, chunk)
        src, dst = (step - 1, step) if way == 0 else (lax.rem(n_g + 1 - step, n_g), n_g - step)
        buffer = line_q if line else keys
        return pltpu.make_async_remote_copy(
            src_ref=buffer.at[src, at],
            dst_ref=buffer.at[dst, at],
            send_sem=ring_send.at[line, way, part, step],
            recv_sem=ring_recv.at[line, way, part, step],
            device_id=(w, right if way == 0 else left),
            device_id_type=MESH,
        )

    def steps_of(line, way, part):
        return half if (way == part) == (line == 0) else half - 1

    def begin(line, part):
        for way in (0, 1):
            ring(line, way, part, 1).start()

    def advance(line, step, part):
        for way in (0, 1):
            if isinstance(step, int) and step > steps_of(line, way, part):
                continue
            ring(line, way, part, step).wait_recv()
            if not isinstance(step, int) or step < steps_of(line, way, part):
                ring(line, way, part, step + 1).start()

    def wide_start(src, dst, k, peer):
        @pl.when(peer != w)
        def _():
            pltpu.make_async_remote_copy(
                src_ref=src.at[peer],
                dst_ref=dst.at[w],
                send_sem=wide_send.at[k],
                recv_sem=wide_recv.at[k],
                device_id=(peer, g),
                device_id_type=MESH,
            ).start()

        @pl.when(peer == w)
        def _():
            pltpu.make_async_copy(src.at[w], dst.at[w], wide_recv.at[k]).start()

    def wide_arrived(dst, k):
        pltpu.make_async_copy(dst, dst, wide_recv.at[k]).wait()

    def wide_drain(src, k):
        others = src.at[pl.ds(0, n_w - 1)]
        pltpu.make_async_copy(others, others, wide_send.at[k]).wait()

    loads[0].wait()
    pl.semaphore_wait(barrier, n_g - 1 + n_w - 1)
    begin(0, 0)
    begin(0, 1)

    owner = lax.broadcasted_iota(jnp.int32, (slots, n_w), 1)
    slot = lax.broadcasted_iota(jnp.int32, (slots, n_w), 0)
    spread = as_bf16(lax.div(slot, cap) == owner)
    picks = send_rows[...]
    high = (picks & ~15).astype(F32).astype(BF16)
    low = (picks & 15).astype(F32).astype(BF16)
    place = lax.broadcasted_iota(jnp.int32, (slots, cap), 1)
    slot = lax.broadcasted_iota(jnp.int32, (slots, cap), 0)
    mine = lax.rem(slot, cap) == place
    high = jnp.where(mine, dot(spread, high, NT), 0.0).astype(BF16)
    low = jnp.where(mine, dot(spread, low, NT), 0.0).astype(BF16)
    ones = jnp.ones((cap, table_rows), BF16)
    row_of = dot(high, ones) + dot(low, ones)
    row = lax.broadcasted_iota(jnp.int32, (slots, table_rows), 1).astype(F32)
    pick = as_bf16(row_of == row)
    loads[2].wait()
    fetched = dot(pick, table[...].astype(BF16)).astype(BF16)
    cold_out[...] = fetched.reshape(n_w, cap, depth)

    loads[1].wait()
    begin(1, 0)

    per = n_w // cold_blocks

    def send_cold(k):
        @pl.loop(0, per)
        def _(j):
            wide_start(cold_out, cold_keys, 0, lax.rem(w + 1 + k * per + j, n_w))

    send_cold(0)
    query_t[...] = jnp.transpose(line_q[0])

    def fold(s, first=False):
        s3 = s.reshape(s.shape[0] // 8, 8, s.shape[1])
        top = jnp.max(s3, axis=0)
        if first:
            top8[...] = top
            sum8[...] = jnp.sum(jnp.exp(s3 - top[None]), axis=0)
        else:
            before = top8[...]
            top = jnp.maximum(before, top)
            top8[...] = top
            sum8[...] = sum8[...] * jnp.exp(before - top) + jnp.sum(jnp.exp(s3 - top[None]), axis=0)

    def score(block, part=None):
        at = slice(None) if part is None else pl.ds(part * chunk, chunk)
        s = dot(keys[block, at], query_t[...]) * scale
        s_in[block, at] = s
        fold(s, first=part is None)

    def score_cold(k):
        at = pl.ds(k * cold_rows, cold_rows)
        owner = lax.broadcasted_iota(jnp.int32, (cold_rows, n_w), 1)
        slot = lax.broadcasted_iota(jnp.int32, (cold_rows, n_w), 0) + k * cold_rows
        spread = as_bf16(lax.div(slot, cap) == owner)
        counts = jnp.broadcast_to(live_counts[...].astype(F32).astype(BF16), (rows, n_w))
        counts = dot(spread, counts, NT)
        place = lax.rem(lax.broadcasted_iota(jnp.int32, (cold_rows, rows), 0), cap).astype(F32)
        owners = pl.ds(k * (n_w // cold_blocks), n_w // cold_blocks)
        found = cold_keys[owners].reshape(cold_rows, depth)
        s = dot(found, query_t[...]) * scale
        s = jnp.where(place < counts, s, -jnp.inf)
        s_cold[at] = s
        fold(s)


    score(0)

    def score_query(step, part):
        for way in (0, 1):
            if isinstance(step, int) and step > steps_of(1, way, part):
                continue
            block = step if way == 0 else n_g - step
            found = line_q[block, pl.ds(part * chunk, chunk)]
            s_back[block, :, pl.ds(part * chunk, chunk)] = dot(keys[0], found, NT) * scale

    looped = max(half - 2, 0)
    cold_first = half - 1 - (cold_blocks + 1) // 2
    in_loop = looped >= cold_blocks and cold_first > (cold_blocks + 1) // 2

    if not in_loop:
        for k in range(1, cold_blocks):
            send_cold(k)

    def items_step(n):
        for part in (0, 1):
            advance(0, n, part)
            if in_loop and not isinstance(n, int):
                k = 2 * (n - 1) + part + 1

                @pl.when(k < cold_blocks)
                def _():
                    send_cold(k)

                if part == 0:

                    @pl.when(n == cold_first)
                    def _():
                        wide_arrived(cold_keys, 0)

                k = 2 * (n - cold_first) + part

                @pl.when((k >= 0) & (k < cold_blocks))
                def _():
                    score_cold(k)

            score(n, part)
            if not isinstance(n, int) or n < half:
                score(n_g - n, part)

    begun = looped // 2

    @pl.loop(0, begun)
    def _(m):
        items_step(2 * m + 1)

        @pl.when(m == 0)
        def _():
            begin(1, 1)

        advance(1, m + 1, 0)
        score_query(m + 1, 0)
        items_step(2 * m + 2)
        advance(1, m + 1, 1)
        score_query(m + 1, 1)

    if begun == 0:
        begin(1, 1)

    if not in_loop:
        wide_arrived(cold_keys, 0)
        for k in range(cold_blocks):
            score_cold(k)

    queue = [(m, part) for m in range(begun + 1, half + 1) for part in (0, 1)]
    passed = []

    def query_step():
        if queue:
            step, part = queue.pop(0)
            advance(1, step, part)
            score_query(step, part)
            passed.append((step, part))

    for n in range(2 * begun + 1, half + 1):
        items_step(n)
        if n < half or half > 2:
            query_step()

    top = jnp.max(top8[...], axis=0, keepdims=True)
    total = jnp.sum(sum8[...] * jnp.exp(top8[...] - top), axis=0, keepdims=True)
    lse_all[0] = top + jnp.log(total)

    def lse_copy(p):
        return pltpu.make_async_remote_copy(
            src_ref=lse_all.at[0],
            dst_ref=lse_all.at[p],
            send_sem=lse_send.at[p],
            recv_sem=lse_recv.at[p],
            device_id=(w, lax.rem(g + p, n_g)),
            device_id_type=MESH,
        )

    @pl.loop(1, n_g)
    def _(p):
        lse_copy(p).start()

    own_part = lax.div(w, per)

    def send_back(i):
        k = lax.rem(own_part + i, cold_blocks)
        at = pl.ds(pl.multiple_of(k * cold_rows, cold_rows), cold_rows)
        d = jnp.exp(s_cold[at] - lse_all[0]).astype(BF16)
        back = (dot(d, line_q[0]) * scale).astype(BF16)
        slot_out[pl.ds(k * per, per)] = back.reshape(per, cap, depth)

        @pl.loop(0, per)
        def _(j):
            wide_start(slot_out, slot_back, 1, k * per + lax.rem(w + j, per))

    for i in range(cold_blocks):
        send_back(i)
        if i % 2 == 1:
            query_step()

    d = jnp.exp(s_in[0] - lse_all[0])
    key = lax.broadcasted_iota(jnp.int32, d.shape, 0)
    query = lax.broadcasted_iota(jnp.int32, d.shape, 1)
    d = (d - jnp.where(key == query, 1.0, 0.0)).astype(BF16)
    query_grad[...] = dot(d, keys[0], TN)
    item_grad[...] = dot(d, line_q[0])

    jobs = n_g - 1 + cold_blocks

    def to_queries(i):
        @pl.when(i < n_g - 1)
        def _():
            d = jnp.exp(s_in[1 + i] - lse_all[0]).astype(BF16)
            query_grad[...] += dot(d, keys[1 + i], TN)

        @pl.when((i >= n_g - 1) & (i < jobs))
        def _():
            k = i - (n_g - 1)
            d = jnp.exp(s_cold[pl.ds(k * cold_rows, cold_rows)] - lse_all[0]).astype(BF16)
            found = cold_keys[pl.ds(k * per, per)].reshape(cold_rows, depth)
            query_grad[...] += dot(d, found, TN)

    def to_items(block):
        d = jnp.exp(s_back[block] - lse_all[block]).astype(BF16)
        item_grad[...] += dot(d, line_q[block])

    owner = lax.broadcasted_iota(jnp.int32, (n_w, slots), 0)
    slot = lax.broadcasted_iota(jnp.int32, (n_w, slots), 1)
    spread = as_bf16(lax.div(slot, cap) == owner)
    picks = send_rows[...]
    high = dot((picks & ~15).astype(F32).astype(BF16), spread)
    low = dot((picks & 15).astype(F32).astype(BF16), spread)
    place = lax.broadcasted_iota(jnp.int32, (cap, slots), 0)
    slot = lax.broadcasted_iota(jnp.int32, (cap, slots), 1)
    row_of = jnp.sum(
        jnp.where(lax.rem(slot, cap) == place, high + low, 0.0), axis=0, keepdims=True
    )
    row = lax.broadcasted_iota(jnp.int32, (table_rows, slots), 0).astype(F32)
    put[...] = as_bf16(row_of == row)

    @pl.loop(1, n_g)
    def _(p):
        lse_copy(p).wait_recv()

    whole = passed[-1][0] - (1 if passed[-1][1] == 0 else 0) if passed else begun
    ready = [(step, n_g - step) for step in range(1, whole + 1)]
    left_over = [jobs * i // max(len(queue) - 1, 1) for i in range(max(len(queue), 1) + 1)]
    turn = 0
    while len(queue) > 1:

        @pl.loop(left_over[turn], left_over[turn + 1])
        def _(i):
            to_queries(i)

        if ready:
            for block in ready.pop(0):
                to_items(block)
        query_step()
        step, part = passed[-1]
        if part == 1:
            ready.append((step, n_g - step))
        turn += 1

    @pl.loop(left_over[turn], jobs)
    def _(i):
        to_queries(i)

    for blocks in ready:
        for block in blocks:
            to_items(block)

    query_grad[...] = query_grad[...] * scale
    saves[0].start()
    def update():
        wide_arrived(slot_back, 1)
        loads[3].wait()
        grad = dot(put[...], slot_back[...].reshape(slots, depth))
        new_table[...] = table[...] - 0.5 * grad / jnp.sqrt(accum[...] + grad * grad)
        saves[2].start()

    update()
    while queue:
        query_step()
    to_items(half)
    item_grad[...] = item_grad[...] * scale
    saves[1].start()

    wide_drain(cold_out, 0)
    wide_drain(slot_out, 1)

    @pl.loop(1, n_g)
    def _(p):
        lse_copy(p).wait_send()

    for way in (0, 1):
        for part in (0, 1):

            for line in (0, 1):

                @pl.loop(1, steps_of(line, way, part) + 1)
                def _(n):
                    ring(line, way, part, n).wait_send()

    for save in saves:
        save.wait()


def store(*refs):
    here, there, held, sems = refs[:3], refs[3:6], refs[6:9], refs[9]
    for i in range(3):
        pltpu.make_async_copy(here[i], held[i], sems.at[0, i]).start()
    for i in range(3):
        pltpu.make_async_copy(here[i], held[i], sems.at[0, i]).wait()
        pltpu.make_async_copy(held[i], there[i], sems.at[1, i]).start()
    for i in range(3):
        pltpu.make_async_copy(held[i], there[i], sems.at[1, i]).wait()


def on_device(n_w, n_g, queries, items, cold_table, accum, send_rows, live_counts):
    rows, depth = queries.shape
    table_rows = cold_table.shape[0]
    cap = send_rows.shape[1]
    slots = n_w * cap
    half = n_g // 2
    vmem = pl.BlockSpec(memory_space=pltpu.VMEM)
    hbm = pl.BlockSpec(memory_space=pl.ANY)
    limit = 60 * 1024 * 1024
    ring_sems = pltpu.SemaphoreType.DMA((2, 2, 2, half + 1))
    results = pl.pallas_call(
        functools.partial(kernel, n_w, n_g, cap),
        out_shape=(
            jax.ShapeDtypeStruct((rows, depth), F32),
            jax.ShapeDtypeStruct((rows, depth), F32),
            jax.ShapeDtypeStruct((table_rows, depth), F32),
        ),
        in_specs=[hbm, hbm, hbm, hbm, vmem, vmem],
        out_specs=(hbm, hbm, hbm),
        scratch_shapes=[
            pltpu.VMEM((rows, depth), F32),
            pltpu.VMEM((rows, depth), F32),
            pltpu.VMEM((table_rows, depth), F32),
            pltpu.VMEM((n_g, rows, depth), BF16),
            pltpu.VMEM((n_g, rows, depth), BF16),
            pltpu.VMEM((n_g, 1, rows), F32),
            pltpu.VMEM((n_g, rows, rows), F32),
            pltpu.VMEM((n_g, rows, rows), F32),
            pltpu.VMEM((slots, rows), F32),
            pltpu.VMEM((8, rows), F32),
            pltpu.VMEM((8, rows), F32),
            pltpu.VMEM((table_rows, depth), F32),
            pltpu.VMEM((table_rows, depth), F32),
            pltpu.VMEM((n_w, cap, depth), BF16),
            pltpu.VMEM((n_w, cap, depth), BF16),
            pltpu.VMEM((n_w, cap, depth), BF16),
            pltpu.VMEM((n_w, cap, depth), BF16),
            pltpu.VMEM((depth, rows), BF16),
            pltpu.VMEM((table_rows, slots), BF16),
            pltpu.SemaphoreType.DMA((4,)),
            pltpu.SemaphoreType.DMA((3,)),
            ring_sems,
            ring_sems,
            pltpu.SemaphoreType.DMA((n_g,)),
            pltpu.SemaphoreType.DMA((n_g,)),
            pltpu.SemaphoreType.DMA((2,)),
            pltpu.SemaphoreType.DMA((2,)),
        ],
        compiler_params=pltpu.CompilerParams(
            collective_id=0, has_side_effects=True, vmem_limit_bytes=limit
        ),
    )(queries, items, cold_table, accum, send_rows.T, live_counts)
    return pl.pallas_call(
        store,
        out_shape=tuple(jax.ShapeDtypeStruct(r.shape, r.dtype) for r in results),
        in_specs=[hbm] * 3,
        out_specs=(hbm,) * 3,
        scratch_shapes=[pltpu.VMEM(r.shape, r.dtype) for r in results]
        + [pltpu.SemaphoreType.DMA((2, 3))],
        compiler_params=pltpu.CompilerParams(vmem_limit_bytes=limit),
    )(*results)


def solution(mesh):
    spec = P(("wide", "group"), None)
    return jax.shard_map(
        functools.partial(on_device, mesh.shape["wide"], mesh.shape["group"]),
        mesh=mesh,
        in_specs=(spec,) * 6,
        out_specs=(spec,) * 3,
        check_vma=False,
    )
```

time: 97.8 us -> 83.1 us (0.85)
  Pallas kernels: 89.9 us -> 82.3 us
  local copies, waits for them, and re-layouts: 6.87 us -> 0 us
    pallas_call x1, Pallas kernels: 89.9 us -> 80.2 us  [on_device(): pl.pallas_call(functools.partial(kernel, n_w, n_g, cap), out_shape=(jax.S...]
    unnamed x14 -> x0, local copies, waits for them, and re-layouts: 6.87 us -> none
    pallas_call x0 -> x1, Pallas kernels: none -> 2.05 us  [on_device(): pl.pallas_call(store, out_shape=tuple((jax.ShapeDtypeStruct(r.shape, r.dt...]
where the time goes in v2:
time: 83.1 us; the launch traced here: 82.9 us
  Pallas kernels  82.3 us (99%)
    pallas_call x1, Pallas kernels, on_device(): pl.pallas_call(functools.partial(kernel, n_w, n_g, cap), out_shape=(jax.S...  80.2 us
    pallas_call x1, Pallas kernels, on_device(): pl.pallas_call(store, out_shape=tuple((jax.ShapeDtypeStruct(r.shape, r.dt...  2.05 us

profile of v2, /device:TPU:8, one launch (start us, length us, event | category | flops | bytes accessed | tf_op | source)
XLA Modules:
  0.0 82.9 jit_solution(2465360671317199236)
XLA Ops:
  0.6 80.2 %shard_map.85 = (f32[256,256]{1,0:T(8,128)}, f32[256,256]{1,0:T(8,128)}, f32[512,256]{1,0:T(8,128)}) custom-call(bf16[256,256]{1,0:T(8,128)(2,1)} %queries.1, bf16[256,256]{1,0:T(8,128)(2,1)} %items.1, f32[512,256]{1,0:T(8,128)} %table_hbm.1, f32[512,256]{1,0:T(8,128)} %accum_hbm.1, s32[16,64]{1,0:T(8,128)} %bitcast.1, s32[1,64]{1,0:T(1,128)} %live_counts.1), custom_call_target="tpu_custom_call" | custom-call | tf_op jit(solution)/shard_map/pallas_call | solution.py:475
  80.8 2.0 %shard_map.86 = (f32[256,256]{1,0:T(8,128)}, f32[256,256]{1,0:T(8,128)}, f32[512,256]{1,0:T(8,128)}) custom-call(f32[256,256]{1,0:T(8,128)} %get-tuple-element.6.refs_0_, f32[256,256]{1,0:T(8,128)} %get-tuple-element.7.refs_1_, f32[512,256]{1,0:T(8,128)} %get-tuple-element.8.refs_2_), custom_call_target="tpu_custom_call" | custom-call | tf_op jit(solution)/shard_map/pallas_call | solution.py:517

commit v3 on v2

--- a/solution.py
+++ b/solution.py
@@ -12,6 +12,8 @@
 TN = (((0,), (0,)), ((), ()))
 F32 = jnp.float32
 BF16 = jnp.bfloat16
+PARTS = 2
+RATE = (1, 2)
 
 
 def dot(a, b, dims=(((1,), (0,)), ((), ()))):
@@ -32,9 +34,6 @@
     accum_hbm,
     send_rows,
     live_counts,
-    query_grad_hbm,
-    item_grad_hbm,
-    new_table_hbm,
     query_grad,
     item_grad,
     new_table,
@@ -55,7 +54,6 @@
     query_t,
     put,
     load_sem,
-    save_sem,
     ring_send,
     ring_recv,
     lse_send,
@@ -67,12 +65,13 @@
     right, left = lax.rem(g + 1, n_g), lax.rem(g + n_g - 1, n_g)
     half = n_g // 2
     rows, depth = queries.shape
-    chunk = rows // 2
+    chunk = rows // PARTS
     slots = n_w * cap
     table_rows = table.shape[0]
     scale = depth ** (-0.5)
     cold_blocks = max(slots // 256, 1)
     cold_rows = slots // cold_blocks
+    per = n_w // cold_blocks
 
     loads = [
         pltpu.make_async_copy(items, keys.at[0], load_sem.at[0]),
@@ -83,12 +82,6 @@
     for load in loads:
         load.start()
 
-    saves = [
-        pltpu.make_async_copy(query_grad, query_grad_hbm, save_sem.at[0]),
-        pltpu.make_async_copy(item_grad, item_grad_hbm, save_sem.at[1]),
-        pltpu.make_async_copy(new_table, new_table_hbm, save_sem.at[2]),
-    ]
-
     barrier = pltpu.get_barrier_semaphore()
 
     @pl.loop(1, n_g)
@@ -104,7 +97,7 @@
         )
 
     def ring(line, way, part, step):
-        at = pl.ds(part * chunk, chunk)
+        at = pl.ds(pl.multiple_of(part * chunk, chunk), chunk)
         src, dst = (step - 1, step) if way == 0 else (lax.rem(n_g + 1 - step, n_g), n_g - step)
         buffer = line_q if line else keys
         return pltpu.make_async_remote_copy(
@@ -117,7 +110,7 @@
         )
 
     def steps_of(line, way, part):
-        return half if (way == part) == (line == 0) else half - 1
+        return half if (way == 0) == ((part < PARTS // 2) == (line == 0)) else half - 1
 
     def begin(line, part):
         for way in (0, 1):
@@ -147,6 +140,12 @@
         def _():
             pltpu.make_async_copy(src.at[w], dst.at[w], wide_recv.at[k]).start()
 
+    def wide_part(src, dst, k, part):
+        @pl.loop(part * per, part * per + per)
+        def _(j):
+            away = (j + 1) // 2
+            wide_start(src, dst, k, lax.rem(w + jnp.where(lax.rem(j, 2) == 0, away, n_w - away), n_w))
+
     def wide_arrived(dst, k):
         pltpu.make_async_copy(dst, dst, wide_recv.at[k]).wait()
 
@@ -156,8 +155,8 @@
 
     loads[0].wait()
     pl.semaphore_wait(barrier, n_g - 1 + n_w - 1)
-    begin(0, 0)
-    begin(0, 1)
+    for part in range(PARTS):
+        begin(0, part)
 
     owner = lax.broadcasted_iota(jnp.int32, (slots, n_w), 1)
     slot = lax.broadcasted_iota(jnp.int32, (slots, n_w), 0)
@@ -179,14 +178,11 @@
     cold_out[...] = fetched.reshape(n_w, cap, depth)
 
     loads[1].wait()
-    begin(1, 0)
-
-    per = n_w // cold_blocks
+    for part in range(PARTS):
+        begin(1, part)
 
     def send_cold(k):
-        @pl.loop(0, per)
-        def _(j):
-            wide_start(cold_out, cold_keys, 0, lax.rem(w + 1 + k * per + j, n_w))
+        wide_part(cold_out, cold_keys, 0, k)
 
     send_cold(0)
     query_t[...] = jnp.transpose(line_q[0])
@@ -203,11 +199,10 @@
             top8[...] = top
             sum8[...] = sum8[...] * jnp.exp(before - top) + jnp.sum(jnp.exp(s3 - top[None]), axis=0)
 
-    def score(block, part=None):
-        at = slice(None) if part is None else pl.ds(part * chunk, chunk)
-        s = dot(keys[block, at], query_t[...]) * scale
-        s_in[block, at] = s
-        fold(s, first=part is None)
+    def score(block, first=False):
+        s = dot(keys[block], query_t[...]) * scale
+        s_in[block] = s
+        fold(s, first)
 
     def score_cold(k):
         at = pl.ds(k * cold_rows, cold_rows)
@@ -225,15 +220,11 @@
         fold(s)
 
 
-    score(0)
-
-    def score_query(step, part):
-        for way in (0, 1):
-            if isinstance(step, int) and step > steps_of(1, way, part):
-                continue
-            block = step if way == 0 else n_g - step
-            found = line_q[block, pl.ds(part * chunk, chunk)]
-            s_back[block, :, pl.ds(part * chunk, chunk)] = dot(keys[0], found, NT) * scale
+    score(0, first=True)
+
+    def score_query(step):
+        for block in {step, n_g - step} if isinstance(step, int) else (step, n_g - step):
+            s_back[block] = dot(keys[0], line_q[block], NT) * scale
 
     looped = max(half - 2, 0)
     cold_first = half - 1 - (cold_blocks + 1) // 2
@@ -243,9 +234,8 @@
         for k in range(1, cold_blocks):
             send_cold(k)
 
-    def items_step(n):
+    def items_work(n):
         for part in (0, 1):
-            advance(0, n, part)
             if in_loop and not isinstance(n, int):
                 k = 2 * (n - 1) + part + 1
 
@@ -265,47 +255,50 @@
                 def _():
                     score_cold(k)
 
-            score(n, part)
-            if not isinstance(n, int) or n < half:
-                score(n_g - n, part)
-
-    begun = looped // 2
-
-    @pl.loop(0, begun)
-    def _(m):
-        items_step(2 * m + 1)
-
-        @pl.when(m == 0)
+        score(n)
+        if not isinstance(n, int) or n < half:
+            score(n_g - n)
+
+    def passed_by(n):
+        return PARTS * n * RATE[0] // RATE[1]
+
+    @pl.loop(1, half - 1)
+    def _(n):
+        for part in range(PARTS):
+            advance(0, n, part)
+
+        @pl.loop(passed_by(n - 1), passed_by(n))
+        def _(e):
+            advance(1, e // PARTS + 1, lax.rem(e, PARTS))
+
+        items_work(n)
+
+        @pl.when(passed_by(n) // PARTS > passed_by(n - 1) // PARTS)
         def _():
-            begin(1, 1)
-
-        advance(1, m + 1, 0)
-        score_query(m + 1, 0)
-        items_step(2 * m + 2)
-        advance(1, m + 1, 1)
-        score_query(m + 1, 1)
-
-    if begun == 0:
-        begin(1, 1)
+            score_query(passed_by(n) // PARTS)
 
     if not in_loop:
         wide_arrived(cold_keys, 0)
         for k in range(cold_blocks):
             score_cold(k)
 
-    queue = [(m, part) for m in range(begun + 1, half + 1) for part in (0, 1)]
-    passed = []
+    events = [(m, part) for m in range(1, half + 1) for part in range(PARTS)]
+    queue = events[passed_by(looped) :]
+    passed = events[: passed_by(looped)]
 
     def query_step():
         if queue:
             step, part = queue.pop(0)
             advance(1, step, part)
-            score_query(step, part)
             passed.append((step, part))
-
-    for n in range(2 * begun + 1, half + 1):
-        items_step(n)
-        if n < half or half > 2:
+            if part == PARTS - 1:
+                score_query(step)
+
+    for n in range(looped + 1, half + 1):
+        for part in range(PARTS):
+            advance(0, n, part)
+        items_work(n)
+        for _ in range(passed_by(n) - passed_by(n - 1)):
             query_step()
 
     top = jnp.max(top8[...], axis=0, keepdims=True)
@@ -326,22 +319,15 @@
     def _(p):
         lse_copy(p).start()
 
-    own_part = lax.div(w, per)
-
-    def send_back(i):
-        k = lax.rem(own_part + i, cold_blocks)
-        at = pl.ds(pl.multiple_of(k * cold_rows, cold_rows), cold_rows)
-        d = jnp.exp(s_cold[at] - lse_all[0]).astype(BF16)
+    @pl.loop(0, cold_blocks)
+    def _(k):
+        d = jnp.exp(s_cold[pl.ds(k * cold_rows, cold_rows)] - lse_all[0]).astype(BF16)
         back = (dot(d, line_q[0]) * scale).astype(BF16)
         slot_out[pl.ds(k * per, per)] = back.reshape(per, cap, depth)
 
-        @pl.loop(0, per)
-        def _(j):
-            wide_start(slot_out, slot_back, 1, k * per + lax.rem(w + j, per))
-
     for i in range(cold_blocks):
-        send_back(i)
-        if i % 2 == 1:
+        wide_part(slot_out, slot_back, 1, i)
+        for _ in range(max(PARTS // 4, 1)):
             query_step()
 
     d = jnp.exp(s_in[0] - lse_all[0])
@@ -388,48 +374,50 @@
     def _(p):
         lse_copy(p).wait_recv()
 
-    whole = passed[-1][0] - (1 if passed[-1][1] == 0 else 0) if passed else begun
+    whole = min(len(passed) // PARTS, half - 1)
     ready = [(step, n_g - step) for step in range(1, whole + 1)]
-    left_over = [jobs * i // max(len(queue) - 1, 1) for i in range(max(len(queue), 1) + 1)]
-    turn = 0
-    while len(queue) > 1:
-
-        @pl.loop(left_over[turn], left_over[turn + 1])
+    turns = max(len(queue) - PARTS // 2, 0)
+    for turn in range(turns):
+
+        @pl.loop(jobs * turn // turns, jobs * (turn + 1) // turns)
         def _(i):
             to_queries(i)
 
-        if ready:
+        query_step()
+        if ready and 2 * turn >= turns * (whole - len(ready)) // max(whole, 1):
             for block in ready.pop(0):
                 to_items(block)
-        query_step()
         step, part = passed[-1]
-        if part == 1:
+        if part == PARTS - 1 and step < half:
             ready.append((step, n_g - step))
-        turn += 1
-
-    @pl.loop(left_over[turn], jobs)
-    def _(i):
-        to_queries(i)
+
+    if turns == 0:
+
+        @pl.loop(0, jobs)
+        def _(i):
+            to_queries(i)
 
     for blocks in ready:
         for block in blocks:
             to_items(block)
 
     query_grad[...] = query_grad[...] * scale
-    saves[0].start()
+
     def update():
         wide_arrived(slot_back, 1)
         loads[3].wait()
         grad = dot(put[...], slot_back[...].reshape(slots, depth))
         new_table[...] = table[...] - 0.5 * grad / jnp.sqrt(accum[...] + grad * grad)
-        saves[2].start()
 
     update()
     while queue:
         query_step()
+        step, part = passed[-1]
+        if part == PARTS - 1 and step < half:
+            to_items(step)
+            to_items(n_g - step)
     to_items(half)
     item_grad[...] = item_grad[...] * scale
-    saves[1].start()
 
     wide_drain(cold_out, 0)
     wide_drain(slot_out, 1)
@@ -439,27 +427,21 @@
         lse_copy(p).wait_send()
 
     for way in (0, 1):
-        for part in (0, 1):
-
+        for part in range(PARTS):
             for line in (0, 1):
 
                 @pl.loop(1, steps_of(line, way, part) + 1)
                 def _(n):
                     ring(line, way, part, n).wait_send()
 
-    for save in saves:
-        save.wait()
-
 
 def store(*refs):
-    here, there, held, sems = refs[:3], refs[3:6], refs[6:9], refs[9]
-    for i in range(3):
-        pltpu.make_async_copy(here[i], held[i], sems.at[0, i]).start()
-    for i in range(3):
-        pltpu.make_async_copy(here[i], held[i], sems.at[0, i]).wait()
-        pltpu.make_async_copy(held[i], there[i], sems.at[1, i]).start()
-    for i in range(3):
-        pltpu.make_async_copy(held[i], there[i], sems.at[1, i]).wait()
+    sems = refs[-1]
+    copies = [pltpu.make_async_copy(refs[i], refs[3 + i], sems.at[i]) for i in range(3)]
+    for copy in copies:
+        copy.start()
+    for copy in copies:
+        copy.wait()
 
 
 def on_device(n_w, n_g, queries, items, cold_table, accum, send_rows, live_counts):
@@ -471,20 +453,17 @@
     vmem = pl.BlockSpec(memory_space=pltpu.VMEM)
     hbm = pl.BlockSpec(memory_space=pl.ANY)
     limit = 60 * 1024 * 1024
-    ring_sems = pltpu.SemaphoreType.DMA((2, 2, 2, half + 1))
+    ring_sems = pltpu.SemaphoreType.DMA((2, 2, PARTS, half + 1))
     results = pl.pallas_call(
         functools.partial(kernel, n_w, n_g, cap),
         out_shape=(
-            jax.ShapeDtypeStruct((rows, depth), F32),
-            jax.ShapeDtypeStruct((rows, depth), F32),
-            jax.ShapeDtypeStruct((table_rows, depth), F32),
-        ),
-        in_specs=[hbm, hbm, hbm, hbm, vmem, vmem],
-        out_specs=(hbm, hbm, hbm),
-        scratch_shapes=[
             pltpu.VMEM((rows, depth), F32),
             pltpu.VMEM((rows, depth), F32),
             pltpu.VMEM((table_rows, depth), F32),
+        ),
+        in_specs=[hbm, hbm, hbm, hbm, vmem, vmem],
+        out_specs=(vmem, vmem, vmem),
+        scratch_shapes=[
             pltpu.VMEM((n_g, rows, depth), BF16),
             pltpu.VMEM((n_g, rows, depth), BF16),
             pltpu.VMEM((n_g, 1, rows), F32),
@@ -502,7 +481,6 @@
             pltpu.VMEM((depth, rows), BF16),
             pltpu.VMEM((table_rows, slots), BF16),
             pltpu.SemaphoreType.DMA((4,)),
-            pltpu.SemaphoreType.DMA((3,)),
             ring_sems,
             ring_sems,
             pltpu.SemaphoreType.DMA((n_g,)),
@@ -519,9 +497,8 @@
         out_shape=tuple(jax.ShapeDtypeStruct(r.shape, r.dtype) for r in results),
         in_specs=[hbm] * 3,
         out_specs=(hbm,) * 3,
-        scratch_shapes=[pltpu.VMEM(r.shape, r.dtype) for r in results]
-        + [pltpu.SemaphoreType.DMA((2, 3))],
-        compiler_params=pltpu.CompilerParams(vmem_limit_bytes=limit),
+        scratch_shapes=[pltpu.SemaphoreType.DMA((3,))],
+        compiler_params=pltpu.CompilerParams(vmem_limit_bytes=4 * 1024 * 1024),
     )(*results)
 
 

time: 83.1 us -> 81.9 us (0.986)
  Pallas kernels: 82.3 us -> 81.1 us
    pallas_call x1, Pallas kernels: 2.05 us -> 0.99 us  [on_device(): pl.pallas_call(store, out_shape=tuple((jax.ShapeDtypeStruct(r.shape, r.dt...]
where the time goes in v3:
time: 81.9 us; the launch traced here: 81.7 us
  Pallas kernels  81.1 us (99%)
    pallas_call x1, Pallas kernels, on_device(): pl.pallas_call(functools.partial(kernel, n_w, n_g, cap), out_shape=(pltpu...  80.1 us

profile of v3, /device:TPU:8, one launch (start us, length us, event | category | flops | bytes accessed | tf_op | source)
XLA Modules:
  0.0 81.7 jit_solution(16554122296064467847)
XLA Ops:
  0.6 80.1 %shard_map.85 = (f32[256,256]{1,0:T(8,128)S(1)}, f32[256,256]{1,0:T(8,128)S(1)}, f32[512,256]{1,0:T(8,128)S(1)}) custom-call(bf16[256,256]{1,0:T(8,128)(2,1)} %queries.1, bf16[256,256]{1,0:T(8,128)(2,1)} %items.1, f32[512,256]{1,0:T(8,128)} %table_hbm.1, f32[512,256]{1,0:T(8,128)} %accum_hbm.1, s32[16,64]{1,0:T(8,128)} %bitcast.1, s32[1,64]{1,0:T(1,128)} %live_counts.1), custom_call_target="tpu_custom_call" | custom-call | tf_op jit(solution)/shard_map/pallas_call | solution.py:457
  80.7 1.0 %shard_map.86 = (f32[256,256]{1,0:T(8,128)}, f32[256,256]{1,0:T(8,128)}, f32[512,256]{1,0:T(8,128)}) custom-call(f32[256,256]{1,0:T(8,128)S(1)} %get-tuple-element.6.refs_0_, f32[256,256]{1,0:T(8,128)S(1)} %get-tuple-element.7.refs_1_, f32[512,256]{1,0:T(8,128)S(1)} %get-tuple-element.8.refs_2_), custom_call_target="tpu_custom_call" | custom-call | tf_op jit(solution)/shard_map/pallas_call | solution.py:495

commit v4 on v3

--- a/solution.py
+++ b/solution.py
@@ -13,7 +13,7 @@
 F32 = jnp.float32
 BF16 = jnp.bfloat16
 PARTS = 2
-RATE = (1, 2)
+RATE = (7, 16)
 
 
 def dot(a, b, dims=(((1,), (0,)), ((), ()))):
@@ -157,6 +157,9 @@
     pl.semaphore_wait(barrier, n_g - 1 + n_w - 1)
     for part in range(PARTS):
         begin(0, part)
+    loads[1].wait()
+    for part in range(PARTS):
+        begin(1, part)
 
     owner = lax.broadcasted_iota(jnp.int32, (slots, n_w), 1)
     slot = lax.broadcasted_iota(jnp.int32, (slots, n_w), 0)
@@ -176,10 +179,6 @@
     loads[2].wait()
     fetched = dot(pick, table[...].astype(BF16)).astype(BF16)
     cold_out[...] = fetched.reshape(n_w, cap, depth)
-
-    loads[1].wait()
-    for part in range(PARTS):
-        begin(1, part)
 
     def send_cold(k):
         wide_part(cold_out, cold_keys, 0, k)

time: 81.9 us -> 82 us (level)
  no operation moved by 1% of the time
where the time goes in v4:
time: 82 us; the launch traced here: 81.8 us
  Pallas kernels  81.2 us (99%)
    pallas_call x1, Pallas kernels, on_device(): pl.pallas_call(functools.partial(kernel, n_w, n_g, cap), out_shape=(pltpu...  80.2 us

profile of v4, /device:TPU:8, one launch (start us, length us, event | category | flops | bytes accessed | tf_op | source)
XLA Modules:
  0.0 81.8 jit_solution(6986474136684345316)
XLA Ops:
  0.6 80.2 %shard_map.85 = (f32[256,256]{1,0:T(8,128)S(1)}, f32[256,256]{1,0:T(8,128)S(1)}, f32[512,256]{1,0:T(8,128)S(1)}) custom-call(bf16[256,256]{1,0:T(8,128)(2,1)} %queries.1, bf16[256,256]{1,0:T(8,128)(2,1)} %items.1, f32[512,256]{1,0:T(8,128)} %table_hbm.1, f32[512,256]{1,0:T(8,128)} %accum_hbm.1, s32[16,64]{1,0:T(8,128)} %bitcast.1, s32[1,64]{1,0:T(1,128)} %live_counts.1), custom_call_target="tpu_custom_call" | custom-call | tf_op jit(solution)/shard_map/pallas_call | solution.py:456
  80.8 1.0 %shard_map.86 = (f32[256,256]{1,0:T(8,128)}, f32[256,256]{1,0:T(8,128)}, f32[512,256]{1,0:T(8,128)}) custom-call(f32[256,256]{1,0:T(8,128)S(1)} %get-tuple-element.6.refs_0_, f32[256,256]{1,0:T(8,128)S(1)} %get-tuple-element.7.refs_1_, f32[512,256]{1,0:T(8,128)S(1)} %get-tuple-element.8.refs_2_), custom_call_target="tpu_custom_call" | custom-call | tf_op jit(solution)/shard_map/pallas_call | solution.py:494
